TPU v7x, 256 devices: a whole 4x4x8 slice. The times are simulated.
256 devices in a mesh: section: 4 (over x_lo, core), seq: 2 (over x_hi), tensor: 32 (over y, z).
Axes of the slice: x: 4 (x_hi: 2, x_lo: 2; x = x_hi * 2 + x_lo), y: 4, z: 8, core: 2. Of those that a mesh axis runs over, the one named last changes fastest.
Arguments:
- grad_out: bfloat16 [6144, 8192], P(('section', 'seq', 'tensor')), parts along dimension 0, may hold values from -6 to 6
- gate_pre: bfloat16 [6144, 26624], P(('section', 'seq'), 'tensor'), parts along dimension 0, may hold values from -6 to 6
- up_pre: bfloat16 [6144, 26624], P(('section', 'seq'), 'tensor'), parts along dimension 0, may hold values from -6 to 6
- down_weight: bfloat16 [106496, 8192], P(('section', 'tensor'), 'seq'), parts along dimension 0, may hold values from -0.0625 to 0.0625
- live_rows: int32 [8], P('section'), parts along dimension 0, may hold values from 96 to 768, as said below
Outputs:
- gate_grad: bfloat16 [6144, 26624], P(('section', 'seq'), 'tensor'), parts along dimension 0
- up_grad: bfloat16 [6144, 26624], P(('section', 'seq'), 'tensor'), parts along dimension 0
There are 4 independent parts, one for each index of `section`. A program takes and returns all parts, laid end to end along the dimension named above; each array names one. Nothing has to cross between parts.
Inputs may be any that keep to these rules, and one draw needn't show every extreme that they name: `live_rows`: in every draw one sequence shard is live in all its 768 rows; the others at least 96.
All inputs are finite; a program needn't handle non-finite values.
Results may differ from a plain program's by a relative error of at most 0.001.
Values may be sent and summed in bfloat16 or wider, within the bound.
A program may use at most 128 MiB of HBM per device.

v0:
```python
import jax
import jax.numpy as jnp
from jax import lax
from jax.sharding import PartitionSpec as P


def finish(hidden_grad, gate_rows, up_rows, live_count):
    row_ids = jnp.arange(hidden_grad.shape[0], dtype=jnp.int32)
    live_mask = (row_ids < live_count).astype(jnp.float32)
    hidden_grad = hidden_grad * live_mask[:, None]
    gate_value = gate_rows.astype(jnp.float32)
    up_value = up_rows.astype(jnp.float32)
    sigmoid_gate = jax.nn.sigmoid(gate_value)
    up_grad = (hidden_grad * gate_value * sigmoid_gate).astype(jnp.bfloat16)
    gate_grad = (
        hidden_grad * up_value * sigmoid_gate * (1.0 + gate_value * (1.0 - sigmoid_gate))
    ).astype(jnp.bfloat16)
    return (gate_grad, up_grad)


def contract(left, right):
    return lax.dot_general(
        left, right, (((1,), (1,)), ((), ())), preferred_element_type=jnp.float32
    )


def shards(grad_out, gate_pre, up_pre, down_weight, live_rows):
    shard_index = lax.axis_index("seq")
    shard_count = live_rows.shape[0]
    live_count = jnp.sum(
        jnp.where(jnp.arange(shard_count, dtype=jnp.int32) == shard_index, live_rows, 0)
    )
    weights_full = lax.all_gather(down_weight, "seq", axis=1, tiled=True)
    all_rows = lax.all_gather(grad_out, "tensor", axis=0, tiled=True)
    return finish(contract(all_rows, weights_full), gate_pre, up_pre, live_count)


def solution(mesh):
    return jax.shard_map(
        shards,
        mesh=mesh,
        in_specs=(
            P(("section", "seq", "tensor"), None),
            P(("section", "seq"), "tensor"),
            P(("section", "seq"), "tensor"),
            P(("section", "tensor"), "seq"),
            P("section"),
        ),
        out_specs=(P(("section", "seq"), "tensor"), P(("section", "seq"), "tensor")),
        check_vma=False,
    )
```

profile of v0, /device:TPU:2, one launch (start us, length us, event | category | flops | bytes accessed | tf_op | source)
XLA Modules:
  0.0 331.2 jit_solution(5456990503519709150)
XLA Ops:
  7.2 0.0 copy-start.2
  7.2 0.0 copy-start.1
  7.2 0.0 copy-start
  7.2 0.0 all-gather.5.cloned.1.call-start
  7.2 0.7 all-gather.5.cloned.1.call-update
  7.9 0.0 all-gather.3.cloned.1.call-start
  8.0 0.7 all-gather.3.cloned.1.call-update
  8.7 0.0 copy-done.2
  8.7 0.6 fusion.9
  9.3 0.6 fusion.8
  10.0 172.6 %all-gather.5.cloned.1.call-done = bf16[832,8192]{1,0:T(8,128)(2,1)} async-done(((bf16[832,4096]{1,0:T(8,128)(2,1)}), bf16[832,8192]{1,0:T(8,128)(2,1)}) %all-gather.5.cloned.1.call-update) | async-done | bytes 13631504 | tf_op jit(solution)/shard_map/all_gather | solution.py:33
  182.5 122.7 %all-gather.3.cloned.1.call-done = bf16[768,8192]{1,0:T(8,128)(2,1)} async-done(((bf16[24,8192]{1,0:T(8,128)(2,1)}), bf16[768,8192]{1,0:T(8,128)(2,1)}) %all-gather.3.cloned.1.call-update) | async-done | bytes 12582928 | tf_op jit(solution)/shard_map/all_gather | solution.py:34
  305.2 0.0 copy-done.1
  305.2 0.0 copy-done
  305.2 19.1 %fusion.7 = (bf16[768,832]{0,1:T(8,128)(2,1)}, bf16[768,832]{0,1:T(8,128)(2,1)}) fusion(bf16[768,832]{0,1:T(8,128)(2,1)S(1)} %copy-done, f32[768]{0:T(1024)S(1)} %fusion.8, bf16[768,832]{0,1:T(8,128)(2,1)S(1)} %copy-done.1, bf16[768,8192]{1,0:T(8,128)(2,1)} %all-gather.3.cloned.1.call-done, bf16[832,8192]{1,0:T(8,128)(2,1)} %all-gather.5.cloned.1.call-done), kind=kOutput, calls=%fused_computation.10 | convolution fusion | flops 10479206400 | bytes 31329280 | tf_op jit(solution)/shard_map/dot_general | solution.py:22
Async XLA Ops:
  7.2 1.5 copy-start.2
  7.2 298.0 %copy-start.1 = (bf16[768,832]{0,1:T(8,128)(2,1)S(1)}, bf16[768,832]{0,1:T(8,128)(2,1)}, u32[]{:S(2)}) copy-start(bf16[768,832]{0,1:T(8,128)(2,1)} %param.7) | copy-start | bytes 3833860
  7.2 298.0 %copy-start = (bf16[768,832]{0,1:T(8,128)(2,1)S(1)}, bf16[768,832]{0,1:T(8,128)(2,1)}, u32[]{:S(2)}) copy-start(bf16[768,832]{0,1:T(8,128)(2,1)} %param.6) | copy-start | bytes 3833860
  7.2 175.3 %all-gather.5.cloned.1.call-start = ((), (), s32[]{:S(2)}) async-start(), calls=%async_computation.1 | async-start | bytes 20447232 | tf_op jit(solution)/shard_map/all_gather | solution.py:33
  7.9 297.3 %all-gather.3.cloned.1.call-start = ((), (), s32[]{:S(2)}) async-start(), calls=%async_computation | async-start | bytes 12976128 | tf_op jit(solution)/shard_map/all_gather | solution.py:34
Sparse Core Ops, SparseCore 0:
  9.8 172.6 all-gather.4
  185.1 120.0 all-gather.2
where the time goes:
time: 332 us; the launch traced here: 331 us
  waiting for transfers between devices  297 us (89%)
  matrix products  19.1 us (6%)
  between operations  14.1 us (4%)
    all_gather x1, waiting for transfers between devices, shards(): weights_full = lax.all_gather(down_weight, 'seq', axis=1, tiled=True)  173 us
    all_gather x1, waiting for transfers between devices, shards(): all_rows = lax.all_gather(grad_out, 'tensor', axis=0, tiled=True)  123 us
    dot_general x1, matrix products, contract(): lax.dot_general(left, right, (((1,), (1,)), ((), ())), preferred_element_...  19.1 us
  transfers between devices with their start and end apart: 2, of which 2 were waited for; matrix products, arithmetic and copies ran while one was open for 0% of the time, Pallas kernels for 0%

commit v1 on v0

v1 whole, which is shorter than its diff:
```python
import functools

import jax
import jax.numpy as jnp
from jax import lax
from jax.experimental import pallas as pl
from jax.experimental.pallas import tpu as pltpu
from jax.sharding import PartitionSpec as P

MESH = pl.DeviceIdType.MESH
NY, NZ = 4, 8
ROWS, FEATS, UNITS = 24, 4096, 832
CUT = 2560
PARTS = ((0, CUT), (CUT, FEATS - CUT))
STEP = 1024
Y_HOPS = (0, 1, 2, -1)
Z_HOPS = (0, 1, 2, 3, 4, -1, -2, -3)
OTHER, OWN = 0, 1
ORDER = (
    104, 120, 72, 88, 1, 5, 8, 24, 33, 37, 40, 56, 2, 6, 9, 25, 34, 38, 48, 29, 3, 7, 13, 26, 35, 39, 10, 4, 45,
    30, 14, 61, 36, 27, 46, 41, 11, 62, 31, -1, 57, 15, 47, 28, 42, 69, 12, 58, 16, 63, 43, 17, 93, 70, 59, 21,
    44, 53, 18, 60, 94, 71, 65, 22, 54, -1, 49, 19, 101, 95, -1, 66, 55, 23, 89, 102, 50, 20, 109, 90, 67, 112,
    103, 73, 125, 51, 77, 110, 91, 68, 126, 74, 52, 111, 78, 92, 97, 127, 75, -1, 98, 79, 117, 76, 105, 121, 80,
    118, 99, 81, 106, 85, 122, 119, 100, 82, 107, 86, 123, -1, 108, 83, 124, 87, 113, 84, -1, 114, -1, 115, 116,
    -1,
)
DEPTH = 1
NEEDS = ((0,), (1, -1), (), (2,))


def packet(code):
    return (code // 64, code // 32 % 2, Y_HOPS[code // 8 % 4], Z_HOPS[code % 8])


def before(hops):
    return hops - 1 if hops > 0 else hops + 1


def origin_of(code):
    whose, part, hy, hz = packet(code)
    along_y = hy != 0 if part == 0 else hz == 0
    if along_y:
        return (whose, part, before(hy), hz), (0, 1 if hy > 0 else -1)
    return (whose, part, hy, before(hz)), (1, 1 if hz > 0 else -1)


def slot_of(name):
    whose, part, hy, hz = name
    return (part, whose, Y_HOPS.index(hy) * NZ + Z_HOPS.index(hz))


def kernel(x_hbm, w_hbm, gate_hbm, up_hbm, live_ref, gate_out, up_out,
           rows, w, gate, up, acc, tiles, arrived, out_g, out_u,
           send_sem, recv_sem, x_send, x_recv, c_send, c_recv, load_sem, out_sem):
    section, q, t = lax.axis_index("section"), lax.axis_index("seq"), lax.axis_index("tensor")
    y, z = t // NZ, t % NZ
    way = 1 - 2 * (section % 2)
    half = y % 2
    partner = (section, 1 - q, t)
    source = (q, 1 - q)

    def neighbour(link):
        axis, sign = link
        step = sign * way
        if axis == 0:
            return (section, q, (y + step + NY) % NY * NZ + z)
        return (section, q, y * NZ + (z + step + NZ) % NZ)

    def region(name):
        whose, part, hy, hz = name
        start, width = PARTS[part]
        shard = q if whose == OWN else 1 - q
        from_y = (y - way * hy + NY) % NY
        from_z = (z - way * hz + NZ) % NZ
        return rows.at[shard, from_y, from_z, :, pl.ds(start, width)]

    def sending(code):
        name, link = origin_of(code)
        here = region(name)
        slot = slot_of(packet(code))
        return pltpu.make_async_remote_copy(
            src_ref=here, dst_ref=here, send_sem=send_sem.at[slot], recv_sem=recv_sem.at[slot],
            device_id=neighbour(link), device_id_type=MESH)

    def receiving(name):
        here = region(name)
        slot = slot_of(name)
        return pltpu.make_async_remote_copy(
            src_ref=here, dst_ref=here, send_sem=send_sem.at[slot], recv_sem=recv_sem.at[slot],
            device_id=partner, device_id_type=MESH)

    def local(part):
        start, width = PARTS[part]
        return pltpu.make_async_copy(
            x_hbm.at[:, pl.ds(pl.multiple_of(q * FEATS + start, 128), width)],
            region((OWN, part, 0, 0)), load_sem.at[part])

    def swap(part):
        start, width = PARTS[part]
        return pltpu.make_async_remote_copy(
            src_ref=x_hbm.at[:, pl.ds(pl.multiple_of((1 - q) * FEATS + start, 128), width)],
            dst_ref=rows.at[q, y, z, :, pl.ds(start, width)],
            send_sem=x_send.at[part], recv_sem=x_recv.at[part], device_id=partner, device_id_type=MESH)

    def swapped(part):
        here = region((OTHER, part, 0, 0))
        return pltpu.make_async_remote_copy(
            src_ref=here, dst_ref=here, send_sem=x_send.at[part], recv_sem=x_recv.at[part],
            device_id=partner, device_id_type=MESH)

    pair, far = 3 * (y // 2), 3 * (1 - y // 2)
    tile_of = (pair + 2 * half, pair + 1, pair + 2 - 2 * half, far + 2 - 2 * half, far + 1, far + 2 * half)

    def exchange(k):
        return pltpu.make_async_remote_copy(
            src_ref=tiles.at[OTHER, tile_of[k]], dst_ref=arrived.at[tile_of[k]],
            send_sem=c_send.at[k], recv_sem=c_recv.at[k], device_id=partner, device_id_type=MESH)

    loads = (pltpu.make_async_copy(w_hbm, w, load_sem.at[2]),
             pltpu.make_async_copy(gate_hbm, gate, load_sem.at[3]),
             pltpu.make_async_copy(up_hbm, up, load_sem.at[4]))
    local(0).start()
    local(1).start()

    barrier = pltpu.get_barrier_semaphore()
    links = ((0, 1), (0, -1), (1, 1), (1, -1))
    for device in [neighbour(link) for link in links] + [partner]:
        pl.semaphore_signal(barrier, inc=1, device_id=device, device_id_type=MESH)
    pl.semaphore_wait(barrier, 5)
    swap(0).start()
    swap(1).start()
    for load in loads:
        load.start()

    actions, stage, waited, queue, block = [[]], [], set(), {link: [] for link in links}, 0
    for code in ORDER:
        if code >= 0:
            name, link = origin_of(code)
            if len(queue[link]) >= DEPTH:
                actions[-1].append(("sent", queue[link].pop(0)))
            if name not in waited:
                waited.add(name)
                actions[-1].append(("arrived", name))
            actions[-1].append(("send", code))
            queue[link].append(code)
        else:
            whose = OTHER if block < 4 else OWN
            for hy in NEEDS[block % 4]:
                for part in (0, 1):
                    for hz in Z_HOPS:
                        name = (whose, part, hy, hz)
                        if name not in waited:
                            waited.add(name)
                            actions[-1].append(("arrived", name))
            block += 1
            actions.append([])
    for action in actions.pop():
        actions[-1].append(action)
    left = [code for link in links for code in queue[link]]

    def act(kind, what):
        if kind == "send":
            sending(what).start()
        elif kind == "sent":
            sending(what).wait_send()
        elif what[2:] != (0, 0):
            receiving(what).wait_recv()
        elif what[0] == OWN:
            local(what[1]).wait()
        else:
            swapped(what[1]).wait_recv()

    def block_of(g, _):
        for b in range(8):
            @pl.when(g == b)
            def _():
                for kind, what in actions[b]:
                    act(kind, what)
                if b == 0:
                    loads[0].wait()
        whose = g // 4
        shard = (1 - whose) * (1 - q) + whose * q
        rank = g % 4
        is1, is2, is3 = rank * (2 - rank) * (3 - rank) // 2, rank * (rank - 1) * (3 - rank) // 2, rank * (rank - 1) * (rank - 2) // 6
        toward = 1 - 2 * half
        from_y = (y + is1 * toward - is2 * toward + is3 * 2 + NY) % NY
        acc[...] = jnp.zeros_like(acc)

        def step(i, _):
            k = pl.multiple_of(i * STEP, STEP)
            block = rows[shard, from_y, :, :, pl.ds(k, STEP)].astype(jnp.float32)
            block = block.reshape(NZ * ROWS, STEP).astype(jnp.bfloat16)
            acc[...] += lax.dot_general(
                w[:, pl.ds(k, STEP)], block, (((1,), (1,)), ((), ())), preferred_element_type=jnp.float32)
            return 0

        lax.fori_loop(0, FEATS // STEP, step, 0)
        first = 3 * (from_y // 2)

        @pl.when(from_y % 2 == 0)
        def _():
            tiles[whose, first] = acc[:, 0:128]
            tiles[whose, first + 1, :, 0:64] = acc[:, 128:192]

        @pl.when(from_y % 2 == 1)
        def _():
            tiles[whose, first + 1, :, 64:128] = acc[:, 0:64]
            tiles[whose, first + 2] = acc[:, 64:192]

        for b, ks in enumerate(((0,), (1, 2), (3,), (4, 5))):
            @pl.when(g == b)
            def _():
                for k in ks:
                    exchange(k).start()
        return 0

    lax.fori_loop(0, 8, block_of, 0)
    for code in left:
        sending(code).wait_send()
    loads[1].wait()
    loads[2].wait()

    live = live_ref[q]
    outs = []
    for k in range(6):
        exchange(k).wait_recv()
        tile = tile_of[k]
        lanes = pl.ds(pl.multiple_of(tile * 128, 128), 128)

        def finish(i, _):
            units = pl.ds(pl.multiple_of(i * 208, 16), 208)
            total = tiles[OWN, tile, units, :] + arrived[tile, units, :]
            row = tile * 128 + lax.broadcasted_iota(jnp.int32, total.shape, 1)
            total = jnp.where(row < live, total, 0.0)
            gate_value = gate[units, lanes].astype(jnp.float32)
            up_value = up[units, lanes].astype(jnp.float32)
            s = jax.nn.sigmoid(gate_value)
            out_u[k, units, :] = (total * gate_value * s).astype(jnp.bfloat16)
            out_g[k, units, :] = (total * up_value * s * (1.0 + gate_value * (1.0 - s))).astype(jnp.bfloat16)
            return 0

        lax.fori_loop(0, UNITS // 208, finish, 0)
        for n, (held, out) in enumerate(((out_g, gate_out), (out_u, up_out))):
            copy = pltpu.make_async_copy(held.at[k], out.at[:, lanes], out_sem.at[n, k])
            copy.start()
            outs.append(copy)
    swap(0).wait_send()
    swap(1).wait_send()
    for k in range(6):
        exchange(k).wait_send()
    for copy in outs:
        copy.wait()


def shards(grad_out, gate_pre, up_pre, down_weight, live_rows):
    anywhere = pl.BlockSpec(memory_space=pl.ANY)
    out = jax.ShapeDtypeStruct((UNITS, NY * NZ * ROWS), jnp.bfloat16)
    gate_grad, up_grad = pl.pallas_call(
        kernel,
        out_shape=(out, out),
        in_specs=[anywhere] * 4 + [pl.BlockSpec(memory_space=pltpu.SMEM)],
        out_specs=(anywhere, anywhere),
        scratch_shapes=[
            pltpu.VMEM((2, NY, NZ, ROWS, FEATS), jnp.bfloat16),
            pltpu.VMEM((UNITS, FEATS), jnp.bfloat16),
            pltpu.VMEM((UNITS, 768), jnp.bfloat16),
            pltpu.VMEM((UNITS, 768), jnp.bfloat16),
            pltpu.VMEM((UNITS, 192), jnp.float32),
            pltpu.VMEM((2, 6, UNITS, 128), jnp.float32),
            pltpu.VMEM((6, UNITS, 128), jnp.float32),
            pltpu.VMEM((6, UNITS, 128), jnp.bfloat16),
            pltpu.VMEM((6, UNITS, 128), jnp.bfloat16),
            pltpu.SemaphoreType.DMA((2, 2, 32)),
            pltpu.SemaphoreType.DMA((2, 2, 32)),
            pltpu.SemaphoreType.DMA((2,)),
            pltpu.SemaphoreType.DMA((2,)),
            pltpu.SemaphoreType.DMA((6,)),
            pltpu.SemaphoreType.DMA((6,)),
            pltpu.SemaphoreType.DMA((5,)),
            pltpu.SemaphoreType.DMA((2, 6)),
        ],
        compiler_params=pltpu.CompilerParams(
            collective_id=0, has_side_effects=True, vmem_limit_bytes=60 * 2**20),
        cost_estimate=pl.CostEstimate(flops=2 * 1536 * 832 * 4096, bytes_accessed=14 * 2**20, transcendentals=768 * 832),
    )(grad_out, down_weight, gate_pre.T, up_pre.T, live_rows)
    return gate_grad.T, up_grad.T


def solution(mesh):
    return jax.shard_map(
        shards,
        mesh=mesh,
        in_specs=(
            P(("section", "seq", "tensor"), None),
            P(("section", "seq"), "tensor"),
            P(("section", "seq"), "tensor"),
            P(("section", "tensor"), "seq"),
            P("section"),
        ),
        out_specs=(P(("section", "seq"), "tensor"), P(("section", "seq"), "tensor")),
        check_vma=False,
    )
```

time: 332 us -> 138 us (0.42)
  waiting for transfers between devices: 297 us -> 0 us
  Pallas kernels: 0 us -> 134 us
  matrix products: 19.1 us -> 0 us
  between operations: 14.1 us -> 0.65 us
  local copies, waits for them, and re-layouts: 0.01 us -> 3.58 us
    all_gather x2 -> x0, waiting for transfers between devices: 295 us -> none  [the longest x1 173 us: shards(): weights_full = lax.all_gather(down_weight, 'seq', axis=1, tiled=True)]
    pallas_call x0 -> x1, Pallas kernels: none -> 134 us  [shards(): pl.pallas_call(kernel, out_shape=(out, out), in_specs=[anywhere] * 4 + [p...]
    dot_general x1 -> x0, matrix products: 19.1 us -> none  [contract(): lax.dot_general(left, right, (((1,), (1,)), ((), ())), preferred_element_...]
    unnamed x6 -> x4, local copies, waits for them, and re-layouts: 0.01 us -> 3.58 us
  transfers between devices with their start and end apart: 2 -> 0, of which waited for: 2 -> 0; matrix products, arithmetic and copies ran while one was open for 0% -> 0% of each run, Pallas kernels for 0% -> 0%
where the time goes in v1:
time: 138 us
  Pallas kernels  134 us (97%)
  local copies, waits for them, and re-layouts  3.58 us (3%)
    pallas_call x1, Pallas kernels, shards(): pl.pallas_call(kernel, out_shape=(out, out), in_specs=[anywhere] * 4 + [p...  134 us
    unnamed x4, local copies, waits for them, and re-layouts  3.58 us

profile of v1, /device:TPU:2, one launch (start us, length us, event | category | flops | bytes accessed | tf_op | source)
XLA Modules:
  0.0 137.9 jit_solution(8761046538704262153)
XLA Ops:
  0.6 133.7 %shard_map.68 = (bf16[832,768]{1,0:T(8,128)(2,1)}, bf16[832,768]{1,0:T(8,128)(2,1)}) custom-call(bf16[24,8192]{1,0:T(8,128)(2,1)} %x_hbm.1, bf16[832,4096]{1,0:T(8,128)(2,1)} %w_hbm.1, bf16[832,768]{1,0:T(8,128)(2,1)} %bitcast.6, bf16[832,768]{1,0:T(8,128)(2,1)} %bitcast.7, s32[2]{0:T(128)} %live_ref.1), custom_call_target="tpu_custom_call" | custom-call | flops 10468982784 | bytes 14680064 | tf_op jit(solution)/shard_map/pallas_call | solution.py:258
  134.3 0.0 copy-start
  134.3 2.5 %copy.9 = bf16[768,832]{0,1:T(8,128)(2,1)} copy(bf16[768,832]{0,1:T(8,128)(2,1)} %bitcast.5) | data formatting | bytes 2555904
  136.9 0.0 copy-done
  136.9 1.0 copy.10
Async XLA Ops:
  134.3 2.5 %copy-start = (bf16[832,768]{1,0:T(8,128)(2,1)S(1)}, bf16[832,768]{1,0:T(8,128)(2,1)}, u32[]{:S(2)}) copy-start(bf16[832,768]{1,0:T(8,128)(2,1)} %get-tuple-element.5) | copy-start | bytes 3833860

commit v2 on v1

--- a/solution.py
+++ b/solution.py
@@ -13,19 +13,20 @@
 CUT = 2560
 PARTS = ((0, CUT), (CUT, FEATS - CUT))
 STEP = 1024
+PIECE = 208
 Y_HOPS = (0, 1, 2, -1)
 Z_HOPS = (0, 1, 2, 3, 4, -1, -2, -3)
 OTHER, OWN = 0, 1
 ORDER = (
-    104, 120, 72, 88, 1, 5, 8, 24, 33, 37, 40, 56, 2, 6, 9, 25, 34, 38, 48, 29, 3, 7, 13, 26, 35, 39, 10, 4, 45,
-    30, 14, 61, 36, 27, 46, 41, 11, 62, 31, -1, 57, 15, 47, 28, 42, 69, 12, 58, 16, 63, 43, 17, 93, 70, 59, 21,
-    44, 53, 18, 60, 94, 71, 65, 22, 54, -1, 49, 19, 101, 95, -1, 66, 55, 23, 89, 102, 50, 20, 109, 90, 67, 112,
-    103, 73, 125, 51, 77, 110, 91, 68, 126, 74, 52, 111, 78, 92, 97, 127, 75, -1, 98, 79, 117, 76, 105, 121, 80,
-    118, 99, 81, 106, 85, 122, 119, 100, 82, 107, 86, 123, -1, 108, 83, 124, 87, 113, 84, -1, 114, -1, 115, 116,
-    -1,
+    104, 69, 97, 120, 101, 65, 88, 72, 8, 24, 1, 5, 112, 109, 121, 93, 40, 37, 33, 56, 77, 70, 66, 9, 29, 6, 2,
+    25, 13, 45, 41, 89, 48, 61, 57, 90, 38, 34, 17, 7, 3, 10, 26, 46, 42, 14, 30, 62, 58, 39, 35, 21, 94, 53, 4,
+    15, 31, 47, 43, 63, 11, 27, 59, 102, 36, 71, 22, 28, -1, -1, 49, 125, 44, 12, 54, 60, -1, 19, 103, 67, -1, 95,
+    18, 110, 50, 126, -1, 23, -1, 55, 105, -1, 20, -1, 98, 16, 117, -1, 91, -1, 68, -1, 111, 74, -1, 51, 127, 85,
+    75, 106, 118, -1, 78, -1, 122, 92, 79, 99, 113, 52, 119, 83, 107, 76, 123, 100, 73, 114, 87, -1, -1, 108, 82,
+    -1, 124, -1, 84, -1, 115, -1, 81, -1, -1, 86, -1, -1, 80, -1, 116, -1, -1, -1, -2, -1, -1, -1, -1,
 )
-DEPTH = 1
 NEEDS = ((0,), (1, -1), (), (2,))
+STEPS = FEATS // STEP
 
 
 def packet(code):
@@ -50,7 +51,7 @@
 
 
 def kernel(x_hbm, w_hbm, gate_hbm, up_hbm, live_ref, gate_out, up_out,
-           rows, w, gate, up, acc, tiles, arrived, out_g, out_u,
+           rows, w, gate, up, acc, tiles, coded, scale, coded_in, scale_in, out_g, out_u,
            send_sem, recv_sem, x_send, x_recv, c_send, c_recv, load_sem, out_sem):
     section, q, t = lax.axis_index("section"), lax.axis_index("seq"), lax.axis_index("tensor")
     y, z = t // NZ, t % NZ
@@ -112,9 +113,27 @@
     tile_of = (pair + 2 * half, pair + 1, pair + 2 - 2 * half, far + 2 - 2 * half, far + 1, far + 2 * half)
 
     def exchange(k):
-        return pltpu.make_async_remote_copy(
-            src_ref=tiles.at[OTHER, tile_of[k]], dst_ref=arrived.at[tile_of[k]],
-            send_sem=c_send.at[k], recv_sem=c_recv.at[k], device_id=partner, device_id_type=MESH)
+        def copy(n, src, dst):
+            return pltpu.make_async_remote_copy(
+                src_ref=src.at[k], dst_ref=dst.at[k], send_sem=c_send.at[n, k], recv_sem=c_recv.at[n, k],
+                device_id=partner, device_id_type=MESH)
+
+        return copy(0, scale, scale_in), copy(1, coded, coded_in)
+
+    def encode(k):
+        tile = tile_of[k]
+
+        def some(i, _):
+            units = pl.ds(pl.multiple_of(i * PIECE, 16), PIECE)
+            part = tiles[OTHER, tile, units, :]
+            row = tile * 128 + lax.broadcasted_iota(jnp.int32, part.shape, 1)
+            part = jnp.where(row < live_ref[1 - q], part, 0.0)
+            most = jnp.maximum(jnp.max(jnp.abs(part), axis=0, keepdims=True), 1e-30)
+            coded[k, units, :] = jnp.round(part * (32767.0 / most)).astype(jnp.int32).astype(jnp.int16)
+            scale[k, i] = jnp.broadcast_to(most * (1.0 / 32767.0), (8, 128))
+            return 0
+
+        lax.fori_loop(0, UNITS // PIECE, some, 0)
 
     loads = (pltpu.make_async_copy(w_hbm, w, load_sem.at[2]),
              pltpu.make_async_copy(gate_hbm, gate, load_sem.at[3]),
@@ -132,37 +151,37 @@
     for load in loads:
         load.start()
 
-    actions, stage, waited, queue, block = [[]], [], set(), {link: [] for link in links}, 0
+    actions, waited, count = [[]], set(), 0
+
+    def need(name):
+        if name not in waited:
+            waited.add(name)
+            actions[-1].append(("arrived", name))
+
     for code in ORDER:
         if code >= 0:
-            name, link = origin_of(code)
-            if len(queue[link]) >= DEPTH:
-                actions[-1].append(("sent", queue[link].pop(0)))
-            if name not in waited:
-                waited.add(name)
-                actions[-1].append(("arrived", name))
+            need(origin_of(code)[0])
             actions[-1].append(("send", code))
-            queue[link].append(code)
+        elif code == -2:
+            actions[-1].append(("finish", (0, 1, 2)))
         else:
-            whose = OTHER if block < 4 else OWN
-            for hy in NEEDS[block % 4]:
-                for part in (0, 1):
-                    for hz in Z_HOPS:
-                        name = (whose, part, hy, hz)
-                        if name not in waited:
-                            waited.add(name)
-                            actions[-1].append(("arrived", name))
-            block += 1
+            block, start = count // STEPS, count % STEPS * STEP
+            for part in (0, 1):
+                low, width = PARTS[part]
+                if low < start + STEP and start < low + width:
+                    for hy in NEEDS[block % 4]:
+                        for hz in Z_HOPS:
+                            need((OTHER if block < 4 else OWN, part, hy, hz))
+            count += 1
             actions.append([])
     for action in actions.pop():
         actions[-1].append(action)
-    left = [code for link in links for code in queue[link]]
 
     def act(kind, what):
         if kind == "send":
             sending(what).start()
-        elif kind == "sent":
-            sending(what).wait_send()
+        elif kind == "finish":
+            finish(what)
         elif what[2:] != (0, 0):
             receiving(what).wait_recv()
         elif what[0] == OWN:
@@ -170,14 +189,41 @@
         else:
             swapped(what[1]).wait_recv()
 
+    live = live_ref[q]
+
+    def result(n, k):
+        lanes = pl.ds(pl.multiple_of(tile_of[k] * 128, 128), 128)
+        return pltpu.make_async_copy(
+            (out_g, out_u)[n].at[k], (gate_out, up_out)[n].at[:, lanes], out_sem.at[n, k])
+
+    def finish(ks):
+        if 0 in ks:
+            loads[1].wait()
+            loads[2].wait()
+        for k in ks:
+            for copy in exchange(k):
+                copy.wait_recv()
+            tile = tile_of[k]
+            lanes = pl.ds(pl.multiple_of(tile * 128, 128), 128)
+
+            def some(i, _):
+                units = pl.ds(pl.multiple_of(i * PIECE, 16), PIECE)
+                theirs = coded_in[k, units, :].astype(jnp.int32).astype(jnp.float32) * scale_in[k, i, 0:1, :]
+                total = tiles[OWN, tile, units, :] + theirs
+                row = tile * 128 + lax.broadcasted_iota(jnp.int32, total.shape, 1)
+                total = jnp.where(row < live, total, 0.0)
+                gate_value = gate[units, lanes].astype(jnp.float32)
+                up_value = up[units, lanes].astype(jnp.float32)
+                s = jax.nn.sigmoid(gate_value)
+                out_u[k, units, :] = (total * gate_value * s).astype(jnp.bfloat16)
+                out_g[k, units, :] = (total * up_value * s * (1.0 + gate_value * (1.0 - s))).astype(jnp.bfloat16)
+                return 0
+
+            lax.fori_loop(0, UNITS // PIECE, some, 0)
+            result(0, k).start()
+            result(1, k).start()
+
     def block_of(g, _):
-        for b in range(8):
-            @pl.when(g == b)
-            def _():
-                for kind, what in actions[b]:
-                    act(kind, what)
-                if b == 0:
-                    loads[0].wait()
         whose = g // 4
         shard = (1 - whose) * (1 - q) + whose * q
         rank = g % 4
@@ -187,6 +233,18 @@
         acc[...] = jnp.zeros_like(acc)
 
         def step(i, _):
+            for b in range(8):
+                @pl.when(g == b)
+                def _():
+                    for c in range(STEPS):
+                        mine = actions[b * STEPS + c]
+                        if mine or b + c == 0:
+                            @pl.when(i == c)
+                            def _():
+                                for kind, what in mine:
+                                    act(kind, what)
+                                if b + c == 0:
+                                    loads[0].wait()
             k = pl.multiple_of(i * STEP, STEP)
             block = rows[shard, from_y, :, :, pl.ds(k, STEP)].astype(jnp.float32)
             block = block.reshape(NZ * ROWS, STEP).astype(jnp.bfloat16)
@@ -194,7 +252,7 @@
                 w[:, pl.ds(k, STEP)], block, (((1,), (1,)), ((), ())), preferred_element_type=jnp.float32)
             return 0
 
-        lax.fori_loop(0, FEATS // STEP, step, 0)
+        lax.fori_loop(0, STEPS, step, 0)
         first = 3 * (from_y // 2)
 
         @pl.when(from_y % 2 == 0)
@@ -211,45 +269,23 @@
             @pl.when(g == b)
             def _():
                 for k in ks:
-                    exchange(k).start()
+                    encode(k)
+                    for copy in exchange(k):
+                        copy.start()
         return 0
 
     lax.fori_loop(0, 8, block_of, 0)
-    for code in left:
-        sending(code).wait_send()
-    loads[1].wait()
-    loads[2].wait()
-
-    live = live_ref[q]
-    outs = []
+    finish((3, 4, 5) if -2 in ORDER else range(6))
+    for code in ORDER:
+        if code >= 0:
+            sending(code).wait_send()
+    for part in (0, 1):
+        swap(part).wait_send()
     for k in range(6):
-        exchange(k).wait_recv()
-        tile = tile_of[k]
-        lanes = pl.ds(pl.multiple_of(tile * 128, 128), 128)
-
-        def finish(i, _):
-            units = pl.ds(pl.multiple_of(i * 208, 16), 208)
-            total = tiles[OWN, tile, units, :] + arrived[tile, units, :]
-            row = tile * 128 + lax.broadcasted_iota(jnp.int32, total.shape, 1)
-            total = jnp.where(row < live, total, 0.0)
-            gate_value = gate[units, lanes].astype(jnp.float32)
-            up_value = up[units, lanes].astype(jnp.float32)
-            s = jax.nn.sigmoid(gate_value)
-            out_u[k, units, :] = (total * gate_value * s).astype(jnp.bfloat16)
-            out_g[k, units, :] = (total * up_value * s * (1.0 + gate_value * (1.0 - s))).astype(jnp.bfloat16)
-            return 0
-
-        lax.fori_loop(0, UNITS // 208, finish, 0)
-        for n, (held, out) in enumerate(((out_g, gate_out), (out_u, up_out))):
-            copy = pltpu.make_async_copy(held.at[k], out.at[:, lanes], out_sem.at[n, k])
-            copy.start()
-            outs.append(copy)
-    swap(0).wait_send()
-    swap(1).wait_send()
-    for k in range(6):
-        exchange(k).wait_send()
-    for copy in outs:
-        copy.wait()
+        for copy in exchange(k):
+            copy.wait_send()
+        result(0, k).wait()
+        result(1, k).wait()
 
 
 def shards(grad_out, gate_pre, up_pre, down_weight, live_rows):
@@ -267,15 +303,18 @@
             pltpu.VMEM((UNITS, 768), jnp.bfloat16),
             pltpu.VMEM((UNITS, 192), jnp.float32),
             pltpu.VMEM((2, 6, UNITS, 128), jnp.float32),
-            pltpu.VMEM((6, UNITS, 128), jnp.float32),
+            pltpu.VMEM((6, UNITS, 128), jnp.int16),
+            pltpu.VMEM((6, UNITS // PIECE, 8, 128), jnp.float32),
+            pltpu.VMEM((6, UNITS, 128), jnp.int16),
+            pltpu.VMEM((6, UNITS // PIECE, 8, 128), jnp.float32),
             pltpu.VMEM((6, UNITS, 128), jnp.bfloat16),
             pltpu.VMEM((6, UNITS, 128), jnp.bfloat16),
             pltpu.SemaphoreType.DMA((2, 2, 32)),
             pltpu.SemaphoreType.DMA((2, 2, 32)),
             pltpu.SemaphoreType.DMA((2,)),
             pltpu.SemaphoreType.DMA((2,)),
-            pltpu.SemaphoreType.DMA((6,)),
-            pltpu.SemaphoreType.DMA((6,)),
+            pltpu.SemaphoreType.DMA((2, 6)),
+            pltpu.SemaphoreType.DMA((2, 6)),
             pltpu.SemaphoreType.DMA((5,)),
             pltpu.SemaphoreType.DMA((2, 6)),
         ],

time: 138 us -> 93.5 us (0.68)
  Pallas kernels: 134 us -> 89.2 us
    pallas_call x1, Pallas kernels: 134 us -> 89.2 us  [shards(): pl.pallas_call(kernel, out_shape=(out, out), in_specs=[anywhere] * 4 + [p...]
where the time goes in v2:
time: 93.5 us; the launch traced here: 93.4 us
  Pallas kernels  89.2 us (95%)
  local copies, waits for them, and re-layouts  3.58 us (4%)
    pallas_call x1, Pallas kernels, shards(): pl.pallas_call(kernel, out_shape=(out, out), in_specs=[anywhere] * 4 + [p...  89.2 us
    unnamed x4, local copies, waits for them, and re-layouts  3.58 us

profile of v2, /device:TPU:2, one launch (start us, length us, event | category | flops | bytes accessed | tf_op | source)
XLA Modules:
  0.0 93.4 jit_solution(1793895961666082050)
XLA Ops:
  0.6 89.2 %shard_map.68 = (bf16[832,768]{1,0:T(8,128)(2,1)}, bf16[832,768]{1,0:T(8,128)(2,1)}) custom-call(bf16[24,8192]{1,0:T(8,128)(2,1)} %x_hbm.1, bf16[832,4096]{1,0:T(8,128)(2,1)} %w_hbm.1, bf16[832,768]{1,0:T(8,128)(2,1)} %bitcast.6, bf16[832,768]{1,0:T(8,128)(2,1)} %bitcast.7, s32[2]{0:T(128)} %live_ref.1), custom_call_target="tpu_custom_call" | custom-call | flops 10468982784 | bytes 14680064 | tf_op jit(solution)/shard_map/pallas_call | solution.py:294
  89.8 0.0 copy-start
  89.8 2.5 %copy.9 = bf16[768,832]{0,1:T(8,128)(2,1)} copy(bf16[768,832]{0,1:T(8,128)(2,1)} %bitcast.5) | data formatting | bytes 2555904
  92.3 0.0 copy-done
  92.3 1.0 %copy.10 = bf16[768,832]{0,1:T(8,128)(2,1)} copy(bf16[768,832]{0,1:T(8,128)(2,1)S(1)} %bitcast.4) | data formatting | bytes 2555904
Async XLA Ops:
  89.8 2.5 %copy-start = (bf16[832,768]{1,0:T(8,128)(2,1)S(1)}, bf16[832,768]{1,0:T(8,128)(2,1)}, u32[]{:S(2)}) copy-start(bf16[832,768]{1,0:T(8,128)(2,1)} %get-tuple-element.5) | copy-start | bytes 3833860

commit v3 on v2

--- a/solution.py
+++ b/solution.py
@@ -10,20 +10,23 @@
 MESH = pl.DeviceIdType.MESH
 NY, NZ = 4, 8
 ROWS, FEATS, UNITS = 24, 4096, 832
-CUT = 2560
-PARTS = ((0, CUT), (CUT, FEATS - CUT))
-STEP = 1024
-PIECE = 208
+CUTS = (2560, 2432)
+PARTS = tuple(((0, cut), (cut, FEATS - cut)) for cut in CUTS)
+LAG = 24
+PARCELS = 4
+STEP = 2048
+PIECE = 64
+PIECES = UNITS // PIECE
 Y_HOPS = (0, 1, 2, -1)
 Z_HOPS = (0, 1, 2, 3, 4, -1, -2, -3)
 OTHER, OWN = 0, 1
 ORDER = (
-    104, 69, 97, 120, 101, 65, 88, 72, 8, 24, 1, 5, 112, 109, 121, 93, 40, 37, 33, 56, 77, 70, 66, 9, 29, 6, 2,
-    25, 13, 45, 41, 89, 48, 61, 57, 90, 38, 34, 17, 7, 3, 10, 26, 46, 42, 14, 30, 62, 58, 39, 35, 21, 94, 53, 4,
-    15, 31, 47, 43, 63, 11, 27, 59, 102, 36, 71, 22, 28, -1, -1, 49, 125, 44, 12, 54, 60, -1, 19, 103, 67, -1, 95,
-    18, 110, 50, 126, -1, 23, -1, 55, 105, -1, 20, -1, 98, 16, 117, -1, 91, -1, 68, -1, 111, 74, -1, 51, 127, 85,
-    75, 106, 118, -1, 78, -1, 122, 92, 79, 99, 113, 52, 119, 83, 107, 76, 123, 100, 73, 114, 87, -1, -1, 108, 82,
-    -1, 124, -1, 84, -1, 115, -1, 81, -1, -1, 86, -1, -1, 80, -1, 116, -1, -1, -1, -2, -1, -1, -1, -1,
+    -4, -4, -4, -4, 65, 120, 101, 69, 72, 104, 97, 88, -4, -4, 1, 5, 8, 24, 121, 102, 73, 89, 33, 56, 37, 40, 66,
+    125, 25, 13, 2, 6, 29, 9, 103, 34, 93, 48, 61, 41, 90, 45, 21, 57, 7, 10, 3, 30, 38, 35, 14, 26, 46, 42, 17,
+    62, 58, 31, 53, 4, 11, 27, 39, 49, 47, 15, 59, 63, 22, 43, 54, 28, -1, 12, 36, 70, 50, 126, 19, 60, 23, 55,
+    44, 18, 109, -1, 20, 51, 94, 67, 71, 80, -1, 127, 105, 16, -1, 110, 52, 77, 112, -1, 98, 78, 95, -1, 91, 68,
+    74, -1, 106, 122, 111, 117, 79, -1, 113, 92, 99, 76, -1, 107, 75, 123, 118, 82, 114, 87, 100, 108, 84, 124,
+    81, 119, 115, 85, -1, 83, -1, 86, -1, 116, -1, -1, -2, -1, -1,
 )
 NEEDS = ((0,), (1, -1), (), (2,))
 STEPS = FEATS // STEP
@@ -51,7 +54,7 @@
 
 
 def kernel(x_hbm, w_hbm, gate_hbm, up_hbm, live_ref, gate_out, up_out,
-           rows, w, gate, up, acc, tiles, coded, scale, coded_in, scale_in, out_g, out_u,
+           rows, w, gate, up, acc, tiles, coded, scale, coded_in, scale_in, up_factor, gate_factor, out_g, out_u,
            send_sem, recv_sem, x_send, x_recv, c_send, c_recv, load_sem, out_sem):
     section, q, t = lax.axis_index("section"), lax.axis_index("seq"), lax.axis_index("tensor")
     y, z = t // NZ, t % NZ
@@ -69,7 +72,7 @@
 
     def region(name):
         whose, part, hy, hz = name
-        start, width = PARTS[part]
+        start, width = PARTS[whose][part]
         shard = q if whose == OWN else 1 - q
         from_y = (y - way * hy + NY) % NY
         from_z = (z - way * hz + NZ) % NZ
@@ -91,13 +94,13 @@
             device_id=partner, device_id_type=MESH)
 
     def local(part):
-        start, width = PARTS[part]
+        start, width = PARTS[OWN][part]
         return pltpu.make_async_copy(
             x_hbm.at[:, pl.ds(pl.multiple_of(q * FEATS + start, 128), width)],
             region((OWN, part, 0, 0)), load_sem.at[part])
 
     def swap(part):
-        start, width = PARTS[part]
+        start, width = PARTS[OTHER][part]
         return pltpu.make_async_remote_copy(
             src_ref=x_hbm.at[:, pl.ds(pl.multiple_of((1 - q) * FEATS + start, 128), width)],
             dst_ref=rows.at[q, y, z, :, pl.ds(start, width)],
@@ -122,22 +125,19 @@
 
     def encode(k):
         tile = tile_of[k]
-
-        def some(i, _):
-            units = pl.ds(pl.multiple_of(i * PIECE, 16), PIECE)
-            part = tiles[OTHER, tile, units, :]
-            row = tile * 128 + lax.broadcasted_iota(jnp.int32, part.shape, 1)
-            part = jnp.where(row < live_ref[1 - q], part, 0.0)
+        row = tile * 128 + lax.broadcasted_iota(jnp.int32, (PIECE, 128), 1)
+        alive = row < live_ref[1 - q]
+        scale[k, 8:16, :] = jnp.zeros((8, 128), jnp.float32)
+        for i in range(PIECES):
+            units = pl.ds(i * PIECE, PIECE)
+            part = jnp.where(alive, tiles[OTHER, tile, units, :], 0.0)
             most = jnp.maximum(jnp.max(jnp.abs(part), axis=0, keepdims=True), 1e-30)
             coded[k, units, :] = jnp.round(part * (32767.0 / most)).astype(jnp.int32).astype(jnp.int16)
-            scale[k, i] = jnp.broadcast_to(most * (1.0 / 32767.0), (8, 128))
-            return 0
-
-        lax.fori_loop(0, UNITS // PIECE, some, 0)
-
-    loads = (pltpu.make_async_copy(w_hbm, w, load_sem.at[2]),
-             pltpu.make_async_copy(gate_hbm, gate, load_sem.at[3]),
-             pltpu.make_async_copy(up_hbm, up, load_sem.at[4]))
+            scale[k, i:i + 1, :] = most * (1.0 / 32767.0)
+
+    weights = pltpu.make_async_copy(w_hbm, w, load_sem.at[2])
+    stored = (pltpu.make_async_copy(gate_hbm, gate, load_sem.at[3]),
+              pltpu.make_async_copy(up_hbm, up, load_sem.at[4]))
     local(0).start()
     local(1).start()
 
@@ -148,10 +148,11 @@
     pl.semaphore_wait(barrier, 5)
     swap(0).start()
     swap(1).start()
-    for load in loads:
+    for load in stored:
         load.start()
-
-    actions, waited, count = [[]], set(), 0
+    weights.start()
+
+    actions, waited, count, flying, factors = [[]], set(), 0, [], 0
 
     def need(name):
         if name not in waited:
@@ -162,12 +163,18 @@
         if code >= 0:
             need(origin_of(code)[0])
             actions[-1].append(("send", code))
+            flying.append(code)
+            if len(flying) > LAG:
+                actions[-1].append(("sent", flying.pop(0)))
         elif code == -2:
             actions[-1].append(("finish", (0, 1, 2)))
+        elif code == -4:
+            actions[-1].append(("factor", factors))
+            factors += 1
         else:
             block, start = count // STEPS, count % STEPS * STEP
             for part in (0, 1):
-                low, width = PARTS[part]
+                low, width = PARTS[OTHER if block < 4 else OWN][part]
                 if low < start + STEP and start < low + width:
                     for hy in NEEDS[block % 4]:
                         for hz in Z_HOPS:
@@ -180,6 +187,10 @@
     def act(kind, what):
         if kind == "send":
             sending(what).start()
+        elif kind == "sent":
+            sending(what).wait_send()
+        elif kind == "factor":
+            factor(what)
         elif kind == "finish":
             finish(what)
         elif what[2:] != (0, 0):
@@ -191,35 +202,40 @@
 
     live = live_ref[q]
 
+    def factor(n):
+        if n == 0:
+            for load in stored:
+                load.wait()
+
+        def some(i, _):
+            units = pl.ds(pl.multiple_of(i * 208, 16), 208)
+            gate_value = gate[units, n * 128:(n + 1) * 128].astype(jnp.float32)
+            up_value = up[units, n * 128:(n + 1) * 128].astype(jnp.float32)
+            s = jax.nn.sigmoid(gate_value)
+            up_factor[n, units, :] = gate_value * s
+            gate_factor[n, units, :] = up_value * s * (1.0 + gate_value * (1.0 - s))
+            return 0
+
+        lax.fori_loop(0, UNITS // 208, some, 0)
+
     def result(n, k):
         lanes = pl.ds(pl.multiple_of(tile_of[k] * 128, 128), 128)
         return pltpu.make_async_copy(
             (out_g, out_u)[n].at[k], (gate_out, up_out)[n].at[:, lanes], out_sem.at[n, k])
 
     def finish(ks):
-        if 0 in ks:
-            loads[1].wait()
-            loads[2].wait()
         for k in ks:
             for copy in exchange(k):
                 copy.wait_recv()
             tile = tile_of[k]
-            lanes = pl.ds(pl.multiple_of(tile * 128, 128), 128)
-
-            def some(i, _):
-                units = pl.ds(pl.multiple_of(i * PIECE, 16), PIECE)
-                theirs = coded_in[k, units, :].astype(jnp.int32).astype(jnp.float32) * scale_in[k, i, 0:1, :]
-                total = tiles[OWN, tile, units, :] + theirs
-                row = tile * 128 + lax.broadcasted_iota(jnp.int32, total.shape, 1)
-                total = jnp.where(row < live, total, 0.0)
-                gate_value = gate[units, lanes].astype(jnp.float32)
-                up_value = up[units, lanes].astype(jnp.float32)
-                s = jax.nn.sigmoid(gate_value)
-                out_u[k, units, :] = (total * gate_value * s).astype(jnp.bfloat16)
-                out_g[k, units, :] = (total * up_value * s * (1.0 + gate_value * (1.0 - s))).astype(jnp.bfloat16)
-                return 0
-
-            lax.fori_loop(0, UNITS // PIECE, some, 0)
+            row = tile * 128 + lax.broadcasted_iota(jnp.int32, (PIECE, 128), 1)
+            alive = row < live
+            for i in range(PIECES):
+                units = pl.ds(i * PIECE, PIECE)
+                theirs = coded_in[k, units, :].astype(jnp.int32).astype(jnp.float32) * scale_in[k, i:i + 1, :]
+                sums = jnp.where(alive, tiles[OWN, tile, units, :] + theirs, 0.0)
+                out_g[k, units, :] = (sums * gate_factor[tile, units, :]).astype(jnp.bfloat16)
+                out_u[k, units, :] = (sums * up_factor[tile, units, :]).astype(jnp.bfloat16)
             result(0, k).start()
             result(1, k).start()
 
@@ -244,7 +260,7 @@
                                 for kind, what in mine:
                                     act(kind, what)
                                 if b + c == 0:
-                                    loads[0].wait()
+                                    weights.wait()
             k = pl.multiple_of(i * STEP, STEP)
             block = rows[shard, from_y, :, :, pl.ds(k, STEP)].astype(jnp.float32)
             block = block.reshape(NZ * ROWS, STEP).astype(jnp.bfloat16)
@@ -276,9 +292,8 @@
 
     lax.fori_loop(0, 8, block_of, 0)
     finish((3, 4, 5) if -2 in ORDER else range(6))
-    for code in ORDER:
-        if code >= 0:
-            sending(code).wait_send()
+    for code in flying:
+        sending(code).wait_send()
     for part in (0, 1):
         swap(part).wait_send()
     for k in range(6):
@@ -288,9 +303,26 @@
         result(1, k).wait()
 
 
+def hand_over(gate_in, up_in, gate_out, up_out, held, in_sem, out_sem):
+    loads, stores = [], []
+    for i in range(PARCELS):
+        units = pl.ds(i * (UNITS // PARCELS), UNITS // PARCELS)
+        for n, (src, dst) in enumerate(((gate_in, gate_out), (up_in, up_out))):
+            loads.append(pltpu.make_async_copy(src.at[units], held.at[n, units], in_sem.at[n, i]))
+            stores.append(pltpu.make_async_copy(held.at[n, units], dst.at[units], out_sem.at[n, i]))
+    for copy in loads:
+        copy.start()
+    for load, store in zip(loads, stores):
+        load.wait()
+        store.start()
+    for copy in stores:
+        copy.wait()
+
+
 def shards(grad_out, gate_pre, up_pre, down_weight, live_rows):
     anywhere = pl.BlockSpec(memory_space=pl.ANY)
     out = jax.ShapeDtypeStruct((UNITS, NY * NZ * ROWS), jnp.bfloat16)
+    tile_set = (6, UNITS, 128)
     gate_grad, up_grad = pl.pallas_call(
         kernel,
         out_shape=(out, out),
@@ -299,16 +331,18 @@
         scratch_shapes=[
             pltpu.VMEM((2, NY, NZ, ROWS, FEATS), jnp.bfloat16),
             pltpu.VMEM((UNITS, FEATS), jnp.bfloat16),
-            pltpu.VMEM((UNITS, 768), jnp.bfloat16),
-            pltpu.VMEM((UNITS, 768), jnp.bfloat16),
+            pltpu.VMEM((UNITS, NY * NZ * ROWS), jnp.bfloat16),
+            pltpu.VMEM((UNITS, NY * NZ * ROWS), jnp.bfloat16),
             pltpu.VMEM((UNITS, 192), jnp.float32),
-            pltpu.VMEM((2, 6, UNITS, 128), jnp.float32),
-            pltpu.VMEM((6, UNITS, 128), jnp.int16),
-            pltpu.VMEM((6, UNITS // PIECE, 8, 128), jnp.float32),
-            pltpu.VMEM((6, UNITS, 128), jnp.int16),
-            pltpu.VMEM((6, UNITS // PIECE, 8, 128), jnp.float32),
-            pltpu.VMEM((6, UNITS, 128), jnp.bfloat16),
-            pltpu.VMEM((6, UNITS, 128), jnp.bfloat16),
+            pltpu.VMEM((2,) + tile_set, jnp.float32),
+            pltpu.VMEM(tile_set, jnp.int16),
+            pltpu.VMEM((6, 16, 128), jnp.float32),
+            pltpu.VMEM(tile_set, jnp.int16),
+            pltpu.VMEM((6, 16, 128), jnp.float32),
+            pltpu.VMEM(tile_set, jnp.float32),
+            pltpu.VMEM(tile_set, jnp.float32),
+            pltpu.VMEM(tile_set, jnp.bfloat16),
+            pltpu.VMEM(tile_set, jnp.bfloat16),
             pltpu.SemaphoreType.DMA((2, 2, 32)),
             pltpu.SemaphoreType.DMA((2, 2, 32)),
             pltpu.SemaphoreType.DMA((2,)),
@@ -322,6 +356,18 @@
             collective_id=0, has_side_effects=True, vmem_limit_bytes=60 * 2**20),
         cost_estimate=pl.CostEstimate(flops=2 * 1536 * 832 * 4096, bytes_accessed=14 * 2**20, transcendentals=768 * 832),
     )(grad_out, down_weight, gate_pre.T, up_pre.T, live_rows)
+    gate_grad, up_grad = pl.pallas_call(
+        hand_over,
+        out_shape=(out, out),
+        in_specs=[anywhere] * 2,
+        out_specs=(anywhere, anywhere),
+        scratch_shapes=[
+            pltpu.VMEM((2, UNITS, NY * NZ * ROWS), jnp.bfloat16),
+            pltpu.SemaphoreType.DMA((2, PARCELS)),
+            pltpu.SemaphoreType.DMA((2, PARCELS)),
+        ],
+        compiler_params=pltpu.CompilerParams(vmem_limit_bytes=60 * 2**20),
+    )(gate_grad, up_grad)
     return gate_grad.T, up_grad.T
 
 

time: 93.5 us -> 91.1 us (0.974)
  local copies, waits for them, and re-layouts: 3.58 us -> 0 us
  Pallas kernels: 89.2 us -> 90.4 us
    unnamed x4 -> x0, local copies, waits for them, and re-layouts: 3.58 us -> none
    pallas_call x0 -> x1, Pallas kernels: none -> 2.57 us  [shards(): pl.pallas_call(hand_over, out_shape=(out, out), in_specs=[anywhere] * 2,...]
    pallas_call x1, Pallas kernels: 89.2 us -> 87.8 us  [shards(): pl.pallas_call(kernel, out_shape=(out, out), in_specs=[anywhere] * 4 + [p...]
where the time goes in v3:
time: 91.1 us; the launch traced here: 91 us
  Pallas kernels  90.4 us (99%)
    pallas_call x1, Pallas kernels, shards(): pl.pallas_call(kernel, out_shape=(out, out), in_specs=[anywhere] * 4 + [p...  87.8 us
    pallas_call x1, Pallas kernels, shards(): pl.pallas_call(hand_over, out_shape=(out, out), in_specs=[anywhere] * 2,...  2.57 us

profile of v3, /device:TPU:2, one launch (start us, length us, event | category | flops | bytes accessed | tf_op | source)
XLA Modules:
  0.0 91.0 jit_solution(16391833433608774190)
XLA Ops:
  0.6 87.8 %shard_map.68 = (bf16[832,768]{1,0:T(8,128)(2,1)}, bf16[832,768]{1,0:T(8,128)(2,1)}) custom-call(bf16[24,8192]{1,0:T(8,128)(2,1)} %x_hbm.1, bf16[832,4096]{1,0:T(8,128)(2,1)} %w_hbm.1, bf16[832,768]{1,0:T(8,128)(2,1)} %bitcast.4, bf16[832,768]{1,0:T(8,128)(2,1)} %bitcast.5, s32[2]{0:T(128)} %live_ref.1), custom_call_target="tpu_custom_call" | custom-call | flops 10468982784 | bytes 14680064 | tf_op jit(solution)/shard_map/pallas_call | solution.py:326
  88.4 2.6 %shard_map.69 = (bf16[832,768]{1,0:T(8,128)(2,1)}, bf16[832,768]{1,0:T(8,128)(2,1)}) custom-call(bf16[832,768]{1,0:T(8,128)(2,1)} %get-tuple-element.6.gate_in, bf16[832,768]{1,0:T(8,128)(2,1)} %get-tuple-element.7.up_in), custom_call_target="tpu_custom_call" | custom-call | tf_op jit(solution)/shard_map/pallas_call | solution.py:359

commit v4 on v3

--- a/solution.py
+++ b/solution.py
@@ -13,7 +13,7 @@
 CUTS = (2560, 2432)
 PARTS = tuple(((0, cut), (cut, FEATS - cut)) for cut in CUTS)
 LAG = 24
-PARCELS = 4
+PARCELS = 2
 STEP = 2048
 PIECE = 64
 PIECES = UNITS // PIECE
@@ -21,12 +21,12 @@
 Z_HOPS = (0, 1, 2, 3, 4, -1, -2, -3)
 OTHER, OWN = 0, 1
 ORDER = (
-    -4, -4, -4, -4, 65, 120, 101, 69, 72, 104, 97, 88, -4, -4, 1, 5, 8, 24, 121, 102, 73, 89, 33, 56, 37, 40, 66,
-    125, 25, 13, 2, 6, 29, 9, 103, 34, 93, 48, 61, 41, 90, 45, 21, 57, 7, 10, 3, 30, 38, 35, 14, 26, 46, 42, 17,
-    62, 58, 31, 53, 4, 11, 27, 39, 49, 47, 15, 59, 63, 22, 43, 54, 28, -1, 12, 36, 70, 50, 126, 19, 60, 23, 55,
-    44, 18, 109, -1, 20, 51, 94, 67, 71, 80, -1, 127, 105, 16, -1, 110, 52, 77, 112, -1, 98, 78, 95, -1, 91, 68,
-    74, -1, 106, 122, 111, 117, 79, -1, 113, 92, 99, 76, -1, 107, 75, 123, 118, 82, 114, 87, 100, 108, 84, 124,
-    81, 119, 115, 85, -1, 83, -1, 86, -1, 116, -1, -1, -2, -1, -1,
+    -4, -4, -4, -4, 65, 69, 101, 104, 120, 97, 72, 88, -4, -4, 1, 24, 5, 8, 105, 109, 112, 56, 33, 70, 40, 93, 66,
+    37, 9, 25, 2, 13, 6, 29, 57, 45, 48, 94, 41, 61, 17, 34, 90, 38, 10, 3, 7, 26, 58, 14, 46, 30, 42, 21, 62, 35,
+    53, 89, 18, 4, 39, 27, 59, 47, 11, 63, 31, 43, 15, 71, 49, -1, 28, 12, 36, 54, 60, 125, 19, 44, 110, 95, 67,
+    102, 23, -1, 50, 55, 22, -1, 126, 20, 121, -1, 16, 103, 98, 91, 74, -1, 111, 51, -1, 127, 68, 77, 78, 117,
+    106, -1, 73, 75, 99, 79, 122, 52, 86, 92, 118, 113, 76, 107, 100, 81, 123, -1, 114, 85, 80, 108, 119, -1, 87,
+    124, -1, 115, 84, -1, 82, 83, -1, 116, -1, -1, -2, -1, -3, -1,
 )
 NEEDS = ((0,), (1, -1), (), (2,))
 STEPS = FEATS // STEP
@@ -168,6 +168,8 @@
                 actions[-1].append(("sent", flying.pop(0)))
         elif code == -2:
             actions[-1].append(("finish", (0, 1, 2)))
+        elif code == -3:
+            actions[-1].append(("finish", (3,)))
         elif code == -4:
             actions[-1].append(("factor", factors))
             factors += 1
@@ -291,7 +293,7 @@
         return 0
 
     lax.fori_loop(0, 8, block_of, 0)
-    finish((3, 4, 5) if -2 in ORDER else range(6))
+    finish((4, 5))
     for code in flying:
         sending(code).wait_send()
     for part in (0, 1):
@@ -303,19 +305,15 @@
         result(1, k).wait()
 
 
-def hand_over(gate_in, up_in, gate_out, up_out, held, in_sem, out_sem):
-    loads, stores = [], []
-    for i in range(PARCELS):
-        units = pl.ds(i * (UNITS // PARCELS), UNITS // PARCELS)
-        for n, (src, dst) in enumerate(((gate_in, gate_out), (up_in, up_out))):
-            loads.append(pltpu.make_async_copy(src.at[units], held.at[n, units], in_sem.at[n, i]))
-            stores.append(pltpu.make_async_copy(held.at[n, units], dst.at[units], out_sem.at[n, i]))
-    for copy in loads:
+def hand_over(gate_in, up_in, gate_out, up_out, sem):
+    copies = []
+    for n, (src, dst) in enumerate(((gate_in, gate_out), (up_in, up_out))):
+        for i in range(PARCELS):
+            units = pl.ds(i * (UNITS // PARCELS), UNITS // PARCELS)
+            copies.append(pltpu.make_async_copy(src.at[units], dst.at[units], sem.at[n, i]))
+    for copy in copies:
         copy.start()
-    for load, store in zip(loads, stores):
-        load.wait()
-        store.start()
-    for copy in stores:
+    for copy in copies:
         copy.wait()
 
 
@@ -325,8 +323,8 @@
     tile_set = (6, UNITS, 128)
     gate_grad, up_grad = pl.pallas_call(
         kernel,
-        out_shape=(out, out),
-        in_specs=[anywhere] * 4 + [pl.BlockSpec(memory_space=pltpu.SMEM)],
+        out_shape=(pltpu.VMEM((UNITS, NY * NZ * ROWS), jnp.bfloat16),) * 2,
+        in_specs=[pl.BlockSpec(memory_space=pltpu.HBM)] * 4 + [pl.BlockSpec(memory_space=pltpu.SMEM)],
         out_specs=(anywhere, anywhere),
         scratch_shapes=[
             pltpu.VMEM((2, NY, NZ, ROWS, FEATS), jnp.bfloat16),
@@ -353,20 +351,16 @@
             pltpu.SemaphoreType.DMA((2, 6)),
         ],
         compiler_params=pltpu.CompilerParams(
-            collective_id=0, has_side_effects=True, vmem_limit_bytes=60 * 2**20),
+            collective_id=0, has_side_effects=True, vmem_limit_bytes=57 * 2**20),
         cost_estimate=pl.CostEstimate(flops=2 * 1536 * 832 * 4096, bytes_accessed=14 * 2**20, transcendentals=768 * 832),
     )(grad_out, down_weight, gate_pre.T, up_pre.T, live_rows)
     gate_grad, up_grad = pl.pallas_call(
         hand_over,
         out_shape=(out, out),
         in_specs=[anywhere] * 2,
-        out_specs=(anywhere, anywhere),
-        scratch_shapes=[
-            pltpu.VMEM((2, UNITS, NY * NZ * ROWS), jnp.bfloat16),
-            pltpu.SemaphoreType.DMA((2, PARCELS)),
-            pltpu.SemaphoreType.DMA((2, PARCELS)),
-        ],
-        compiler_params=pltpu.CompilerParams(vmem_limit_bytes=60 * 2**20),
+        out_specs=(pl.BlockSpec(memory_space=pltpu.HBM),) * 2,
+        scratch_shapes=[pltpu.SemaphoreType.DMA((2, PARCELS))],
+        compiler_params=pltpu.CompilerParams(vmem_limit_bytes=2**20),
     )(gate_grad, up_grad)
     return gate_grad.T, up_grad.T
 

time: 91.1 us -> 89 us (0.977)
  Pallas kernels: 90.4 us -> 88.3 us
    pallas_call x1, Pallas kernels: 2.57 us -> 1.5 us  [shards(): pl.pallas_call(hand_over, out_shape=(out, out), in_specs=[anywhere] * 2,...]
    pallas_call x1, Pallas kernels: 87.8 us -> 86.8 us  [shards(): pl.pallas_call(kernel, out_shape=(pltpu.VMEM((UNITS, NY * NZ * ROWS), jnp...]
where the time goes in v4:
time: 89 us; the launch traced here: 88.9 us
  Pallas kernels  88.3 us (99%)
    pallas_call x1, Pallas kernels, shards(): pl.pallas_call(kernel, out_shape=(pltpu.VMEM((UNITS, NY * NZ * ROWS), jnp...  86.8 us

profile of v4, /device:TPU:2, one launch (start us, length us, event | category | flops | bytes accessed | tf_op | source)
XLA Modules:
  0.0 88.9 jit_solution(7947166008691340595)
XLA Ops:
  0.6 86.8 %shard_map.68 = (bf16[832,768]{1,0:T(8,128)(2,1)S(1)}, bf16[832,768]{1,0:T(8,128)(2,1)S(1)}) custom-call(bf16[24,8192]{1,0:T(8,128)(2,1)} %x_hbm.1, bf16[832,4096]{1,0:T(8,128)(2,1)} %w_hbm.1, bf16[832,768]{1,0:T(8,128)(2,1)} %bitcast.4, bf16[832,768]{1,0:T(8,128)(2,1)} %bitcast.5, s32[2]{0:T(128)} %live_ref.1), custom_call_target="tpu_custom_call" | custom-call | flops 10468982784 | bytes 14680064 | tf_op jit(solution)/shard_map/pallas_call | solution.py:324
  87.4 1.5 %shard_map.69 = (bf16[832,768]{1,0:T(8,128)(2,1)}, bf16[832,768]{1,0:T(8,128)(2,1)}) custom-call(bf16[832,768]{1,0:T(8,128)(2,1)S(1)} %get-tuple-element.6.gate_in, bf16[832,768]{1,0:T(8,128)(2,1)S(1)} %get-tuple-element.7.up_in), custom_call_target="tpu_custom_call" | custom-call | tf_op jit(solution)/shard_map/pallas_call | solution.py:357
